TPU v7x, 32 devices: a whole 2x2x4 slice. The times are simulated.
32 devices in a mesh: rec: 2 (over y), leaf: 4 (over z), rhs: 2 (over x), pan: 2 (over core).
Axes of the slice: x: 2, y: 2, z: 4, core: 2. Of those that a mesh axis runs over, the one named last changes fastest.
Arguments:
- bottom_source: bfloat16 [32768, 256], P(('rec', 'leaf', 'rhs', 'pan')), parts along dimension 0, may hold values from -6 to 6
- bottom_inverse: bfloat16 [32768, 1024], P(('rec', 'leaf', 'rhs', 'pan')), parts along dimension 0, as said below
- bottom_update: bfloat16 [4096, 1024], P(('rec', 'leaf', 'rhs', 'pan')), parts along dimension 0, may hold values from -0.0625 to 0.0625
- bottom_sensitivity: bfloat16 [1024, 16384], P('rec', ('leaf', 'rhs', 'pan')), parts along dimension 0, may hold values from -0.03125 to 0.03125
- bottom_order: int32 [16, 1024], P(('leaf', 'rhs', 'pan')), may hold values from 0 to 1023, each once within a row
- bottom_extent: int32 [16], P(('leaf', 'rhs', 'pan')), may hold values from 384 to 1024, as said below
- bottom_targets: int32 [16, 128], P(('leaf', 'rhs', 'pan')), may hold values from 0 to 255, as said below
- upper_source: bfloat16 [3584, 256], P(('rec', 'leaf'), ('rhs', 'pan')), parts along dimension 0, may hold values from -6 to 6
- upper_inverse: bfloat16 [3584, 256], P(('rec', 'leaf')), parts along dimension 0, as said below
- upper_update: bfloat16 [256, 1536], P('rec', 'leaf'), parts along dimension 0, may hold values from -0.25 to 0.25
- upper_targets: int32 [6, 128], replicated, may hold values from 0 to 255, as said below
Outputs:
- adjoint: bfloat16 [32768, 256], P(('rec', 'leaf', 'rhs', 'pan')), parts along dimension 0
- gradient: float32 [1024, 256], P(('rec', 'leaf', 'rhs', 'pan')), parts along dimension 0
There are 2 independent parts, one for each index of `rec`. A program takes and returns all parts, laid end to end along the dimension named above; an argument that names none is the same for every part. Nothing has to cross between parts.
Inputs may be any that keep to these rules, and one draw needn't show every extreme that they name: `bottom_inverse`: lower triangular, with its diagonal between 0.6 and 1.4. `upper_inverse`: lower triangular in each front's row order, with its diagonal between 0.6 and 1.4. `bottom_extent`: a multiple of 128; some front uses all 1024 rows. `bottom_targets`: the rows of one front go to distinct rows. `upper_targets`: the rows of one front go to distinct rows.
All inputs are finite; a program needn't handle non-finite values.
Results may differ from a plain program's by a relative error of at most 0.0058.
Values may be sent and summed in bfloat16 or wider, within the bound.
A program may use at most 64 MiB of HBM per device.

v0:
```python
import jax
import jax.numpy as jnp
from jax import lax
from jax.sharding import PartitionSpec as P


def partner(value, axis, apart):
    mask = 2**apart
    pairs = [(source, source ^ mask) for source in range(lax.axis_size(axis))]
    return lax.ppermute(value, axis, pairs)


def climb_sum(values, bit_count):
    for bit_index in range(bit_count):
        values = values + partner(values, "leaf", bit_index)
    return values


def descend_sum(values, bit_count):
    for bit_index in range(bit_count):
        values = values + partner(values, "leaf", bit_index)
    return values


def shards(
    bottom_source,
    bottom_inverse,
    bottom_update,
    bottom_sensitivity,
    bottom_order,
    bottom_extent,
    bottom_targets,
    upper_source,
    upper_inverse,
    upper_update,
    upper_targets,
):
    leaves = lax.axis_size("leaf")
    depth = leaves.bit_length() - 1
    leaf_place = lax.axis_index("leaf")
    front_rows = bottom_inverse.shape[0]
    front_size = upper_inverse.shape[1]
    order_rows = bottom_order[0]
    row_mask = (jnp.arange(front_rows, dtype=jnp.int32) < bottom_extent[0]).astype(jnp.bfloat16)[
        :, None
    ]
    ordered = bottom_source[order_rows] * row_mask
    solved = (
        jnp.dot(bottom_inverse, ordered, preferred_element_type=jnp.float32) * row_mask
    ).astype(jnp.bfloat16)
    contrib = jnp.dot(bottom_update, solved, preferred_element_type=jnp.float32)
    spread = (
        jnp.zeros((front_size, contrib.shape[1]), jnp.float32).at[bottom_targets[0]].set(contrib)
    )
    summed = lax.psum(spread, ("rhs", "pan"))
    loads = lax.all_gather(upper_source, ("rhs", "pan"), axis=1, tiled=True)
    column_count = summed.shape[1]
    front_input = (loads[0:front_size].astype(jnp.float32) - summed).astype(jnp.bfloat16)
    solved_upper = []
    for height in range(depth + 1):
        row_count = front_size >> height
        offset = 2 * front_size - (2 * front_size >> height)
        inverse_now = upper_inverse[offset : offset + row_count]
        solved_front = jnp.dot(inverse_now, front_input, preferred_element_type=jnp.float32).astype(
            jnp.bfloat16
        )
        solved_upper.append(solved_front)
        if height < depth:
            update_now = upper_update[:, offset : offset + row_count]
            lifted = jnp.dot(update_now, solved_front, preferred_element_type=jnp.float32)
            map_row = 2 * leaves - (2 * leaves >> height) + leaf_place // (1 << height)
            targets = lax.dynamic_slice_in_dim(upper_targets, map_row, 1, 0)[0]
            partial_input = (
                jnp.zeros((front_size, column_count), jnp.float32).at[targets].set(-lifted)
            )
            parent_rows = front_size >> height + 1
            parent_offset = 2 * front_size - (2 * front_size >> height + 1)
            parent_place = leaf_place % (2 << height) * parent_rows
            own_load = loads[parent_offset : parent_offset + parent_rows].astype(jnp.float32)
            current = lax.dynamic_slice_in_dim(partial_input, parent_place, parent_rows, 0)
            partial_input = lax.dynamic_update_slice_in_dim(
                partial_input, current + own_load, parent_place, 0
            )
            front_input = climb_sum(partial_input, height + 1).astype(jnp.bfloat16)
    back_rows = None
    for height in range(depth, -1, -1):
        row_count = front_size >> height
        offset = 2 * front_size - (2 * front_size >> height)
        inverse_now = upper_inverse[offset : offset + row_count]
        if height == depth:
            residue = solved_upper[height]
        else:
            map_row = 2 * leaves - (2 * leaves >> height) + leaf_place // (1 << height)
            targets = lax.dynamic_slice_in_dim(upper_targets, map_row, 1, 0)[0]
            picked = back_rows[targets]
            update_now = upper_update[:, offset : offset + row_count]
            coupled = jnp.einsum(
                "rj,rc->jc", update_now, picked, preferred_element_type=jnp.float32
            )
            residue = (solved_upper[height].astype(jnp.float32) - coupled).astype(jnp.bfloat16)
        partial_back = jnp.einsum(
            "ij,ic->jc", inverse_now, residue, preferred_element_type=jnp.float32
        )
        back_rows = descend_sum(partial_back, height).astype(jnp.bfloat16)
    picked_root = back_rows[bottom_targets[0]]
    coupled_root = jnp.einsum(
        "rj,rc->jc", bottom_update, picked_root, preferred_element_type=jnp.float32
    )
    bottom_residue = ((solved.astype(jnp.float32) - coupled_root) * row_mask).astype(jnp.bfloat16)
    bottom_back = (
        jnp.einsum("ij,ic->jc", bottom_inverse, bottom_residue, preferred_element_type=jnp.float32)
        * row_mask
    ).astype(jnp.bfloat16)
    adjoint = jnp.zeros_like(bottom_back).at[order_rows].set(bottom_back)
    gradient = lax.psum_scatter(
        -jnp.dot(bottom_sensitivity, adjoint, preferred_element_type=jnp.float32),
        ("leaf", "rhs", "pan"),
        scatter_dimension=0,
        tiled=True,
    )
    return (adjoint, gradient)


def solution(mesh):
    placed = (
        P(("rec", "leaf", "rhs", "pan"), None),
        P(("rec", "leaf", "rhs", "pan"), None),
        P(("rec", "leaf", "rhs", "pan"), None),
        P("rec", ("leaf", "rhs", "pan")),
        P(("leaf", "rhs", "pan"), None),
        P(("leaf", "rhs", "pan")),
        P(("leaf", "rhs", "pan"), None),
        P(("rec", "leaf"), ("rhs", "pan")),
        P(("rec", "leaf"), None),
        P("rec", "leaf"),
        P(),
    )
    return jax.shard_map(
        shards,
        mesh=mesh,
        in_specs=placed,
        out_specs=(P(("rec", "leaf", "rhs", "pan"), None), P(("rec", "leaf", "rhs", "pan"), None)),
        check_vma=False,
    )
```

profile of v0, /device:TPU:0, one launch (start us, length us, event | category | flops | bytes accessed | tf_op | source)
XLA Modules:
  0.0 189.3 jit_solution(15696807839329698646)
XLA Ops:
  9.4 4.6 %gather_fusion = bf16[1024,256]{1,0:T(8,128)(2,1)S(1)} fusion(bf16[1024,256]{1,0:T(8,128)(2,1)} %param.11, s32[1024]{0:T(1024)S(1)} %broadcast_clamp_fusion), kind=kCustom, calls=%fused_computation | custom fusion | bytes 1052672 | tf_op jit(solution)/shard_map/gather | solution.py:47
  14.0 1.0 fusion.3
  15.0 0.8 copy-done.3
  16.2 1.7 scatter_custom_fusion
  18.0 7.2 %all_gather.3 = bf16[448,256]{0,1:T(8,128)(2,1)S(1)} all-gather(bf16[448,64]{0,1:T(8,128)(2,1)S(1)} %copy-done.7), channel_id=1, replica_groups=mesh['rec'=2,'leaf'=4,'rhs'=2,'pan'=2] {'rhs','pan'}, dimensions={1}, use_global_device_ids=true | all-gather | bytes 286720 | tf_op jit(solution)/shard_map/all_gather | solution.py:56
  25.5 0.8 fusion.45
  26.3 26.5 %all-reduce.2.cloned.1.call-done = f32[256,256]{1,0:T(8,128)} async-done(((f32[256,256]{1,0:T(8,128)}), f32[256,256]{1,0:T(8,128)}) %all-reduce.2.cloned.1.call-update) | async-done | bytes 262160 | tf_op jit(solution)/shard_map/psum | solution.py:55
  52.8 1.2 convolution_convert_fusion.1
  54.2 1.1 scatter_custom_fusion.1
  55.4 1.6 collective-permute-start
  57.0 5.1 %collective-permute-done = f32[256,256]{1,0:T(8,128)S(1)} collective-permute-done((f32[256,256]{1,0:T(8,128)S(1)}, f32[256,256]{1,0:T(8,128)S(1)}, u32[]{:S(2)}, u32[]{:S(2)}) %collective-permute-start) | collective-permute-done | bytes 262176 | tf_op jit(solution)/shard_map/ppermute | solution.py:10
  62.6 1.1 scatter_custom_fusion.2
  63.7 1.8 collective-permute-start.1
  65.5 4.6 %collective-permute-done.1 = f32[256,256]{1,0:T(8,128)S(1)} collective-permute-done((f32[256,256]{1,0:T(8,128)S(1)}, f32[256,256]{1,0:T(8,128)S(1)}, u32[]{:S(2)}, u32[]{:S(2)}) %collective-permute-start.1) | collective-permute-done | bytes 262176 | tf_op jit(solution)/shard_map/ppermute | solution.py:10
  70.2 3.3 %collective-permute-start.2 = (f32[256,256]{1,0:T(8,128)S(1)}, f32[256,256]{1,0:T(8,128)S(1)}, u32[]{:S(2)}, u32[]{:S(2)}) collective-permute-start(f32[256,256]{1,0:T(8,128)S(1)} %add.117), channel_id=1, source_target_pairs={{0,8},{4,12},{8,0},{12,4},{1,9},{5,13},{9,1},{13,5},{2,10},{6,14},... | collective-permute-start | bytes 786440 | tf_op jit(solution)/shard_map/ppermute | solution.py:10
  73.5 8.1 %collective-permute-done.2 = f32[256,256]{1,0:T(8,128)S(1)} collective-permute-done((f32[256,256]{1,0:T(8,128)S(1)}, f32[256,256]{1,0:T(8,128)S(1)}, u32[]{:S(2)}, u32[]{:S(2)}) %collective-permute-start.2) | collective-permute-done | bytes 262176 | tf_op jit(solution)/shard_map/ppermute | solution.py:10
  82.0 0.8 collective-permute-start.3
  82.8 5.6 %collective-permute-done.3 = f32[256,256]{0,1:T(8,128)S(1)} collective-permute-done((f32[256,256]{0,1:T(8,128)S(1)}, f32[256,256]{0,1:T(8,128)S(1)}, u32[]{:S(2)}, u32[]{:S(2)}) %collective-permute-start.3) | collective-permute-done | bytes 262176 | tf_op jit(solution)/shard_map/ppermute | solution.py:10
  88.5 2.8 %collective-permute-start.4 = (f32[256,256]{0,1:T(8,128)S(1)}, f32[256,256]{0,1:T(8,128)S(1)}, u32[]{:S(2)}, u32[]{:S(2)}) collective-permute-start(f32[256,256]{0,1:T(8,128)S(1)} %add.119), channel_id=1, source_target_pairs={{0,8},{4,12},{8,0},{12,4},{1,9},{5,13},{9,1},{13,5},{2,10},{6,14},... | collective-permute-start | bytes 786440 | tf_op jit(solution)/shard_map/ppermute | solution.py:10
  91.3 9.9 %collective-permute-done.4 = f32[256,256]{0,1:T(8,128)S(1)} collective-permute-done((f32[256,256]{0,1:T(8,128)S(1)}, f32[256,256]{0,1:T(8,128)S(1)}, u32[]{:S(2)}, u32[]{:S(2)}) %collective-permute-start.4) | collective-permute-done | bytes 262176 | tf_op jit(solution)/shard_map/ppermute | solution.py:10
  101.3 0.8 gather_fusion.1
  102.2 1.1 convolution_bitcast_fusion
  103.3 0.8 collective-permute-start.5
  104.1 6.5 %collective-permute-done.5 = f32[256,256]{0,1:T(8,128)S(1)} collective-permute-done((f32[256,256]{0,1:T(8,128)S(1)}, f32[256,256]{0,1:T(8,128)S(1)}, u32[]{:S(2)}, u32[]{:S(2)}) %collective-permute-start.5) | collective-permute-done | bytes 262176 | tf_op jit(solution)/shard_map/ppermute | solution.py:10
  110.8 0.8 gather_fusion.2
  111.6 1.2 fusion.7
  112.9 0.8 gather_fusion.3
  113.8 1.8 fusion.4
  115.8 5.1 %scatter_custom_fusion.3 = bf16[1024,256]{1,0:T(8,128)(2,1)S(1)} fusion(s32[1024]{0:T(1024)S(1)} %bitcast.59, bf16[1024,256]{1,0:T(8,128)(2,1)S(1)} %copy.36, bf16[]{:T(256)} %constant.56.clone.1), kind=kCustom, calls=%fused_computation.42 | custom fusion | bytes 524290 | tf_op jit(solution)/shard_map/scatter | solution.py:114
  120.9 1.9 %fusion.5 = f32[512,256]{0,1:T(8,128)S(1)} fusion(bf16[1024,256]{1,0:T(8,128)(2,1)S(1)} %scatter_custom_fusion.3, bf16[512,1024]{1,0:T(8,128)(2,1)} %param.14), kind=kOutput, calls=%fused_computation.17 | convolution fusion | flops 268566528 | bytes 2097152 | tf_op jit(solution)/shard_map/dot_general | solution.py:116
  122.8 1.0 copy.38
  123.9 58.6 %reduce-scatter.4.cloned.1.call-done = f32[32,256]{1,0:T(8,128)} async-done(((f32[512,256]{1,0:T(8,128)}), f32[32,256]{1,0:T(8,128)}) %reduce-scatter.4.cloned.1.call-update) | async-done | bytes 32784
  (50 shorter events, 4.1 us)
Async XLA Ops:
  7.2 6.8 %copy-start = (bf16[1024,1024]{1,0:T(8,128)(2,1)S(1)}, bf16[1024,1024]{1,0:T(8,128)(2,1)}, u32[]{:S(2)}) copy-start(bf16[1024,1024]{1,0:T(8,128)(2,1)} %param.12) | copy-start | bytes 6291460
  7.2 45.6 %all-reduce.2.cloned.1.call-start = ((), (), s32[]{:S(2)}) async-start(), calls=%async_computation.1 | async-start | bytes 524288 | tf_op jit(solution)/shard_map/psum | solution.py:55
  14.0 1.8 copy-start.6
  14.0 4.0 %copy-start.7 = (bf16[448,64]{0,1:T(8,128)(2,1)S(1)}, bf16[448,64]{0,1:T(8,128)(2,1)}, u32[]{:S(2)}) copy-start(bf16[448,64]{0,1:T(8,128)(2,1)} %param.18) | copy-start | bytes 172036
  15.0 0.8 copy-start.3
  15.8 36.9 %copy-start.2 = (bf16[448,256]{1,0:T(8,128)(2,1)S(1)}, bf16[448,256]{1,0:T(8,128)(2,1)}, u32[]{:S(2)}) copy-start(bf16[448,256]{1,0:T(8,128)(2,1)} %param.19) | copy-start | bytes 688132
  15.8 38.1 %copy-start.5 = (bf16[128,384]{1,0:T(8,128)(2,1)S(1)}, bf16[128,384]{1,0:T(8,128)(2,1)}, u32[]{:S(2)}) copy-start(bf16[128,384]{1,0:T(8,128)(2,1)} %param.20) | copy-start | bytes 294916
  17.9 164.5 %reduce-scatter.4.cloned.1.call-start = ((), (), s32[]{:S(2)}) async-start(), calls=%async_computation.2 | async-start | bytes 557056
  55.4 6.7 %collective-permute-start = (f32[256,256]{1,0:T(8,128)S(1)}, f32[256,256]{1,0:T(8,128)S(1)}, u32[]{:S(2)}, u32[]{:S(2)}) collective-permute-start(f32[256,256]{1,0:T(8,128)S(1)} %add_dynamic-update-slice_fusion), channel_id=1, source_target_pairs={{0,4},{4,0},{8,12},{12,8},{1,5},{5,1},{9,13},{13,9},{2,6},{6,2},{1... | collective-permute-start | bytes 786440 | tf_op jit(solution)/shard_map/ppermute | solution.py:10
  63.7 6.4 %collective-permute-start.1 = (f32[256,256]{1,0:T(8,128)S(1)}, f32[256,256]{1,0:T(8,128)S(1)}, u32[]{:S(2)}, u32[]{:S(2)}) collective-permute-start(f32[256,256]{1,0:T(8,128)S(1)} %add_dynamic-update-slice_fusion.1), channel_id=1, source_target_pairs={{0,4},{4,0},{8,12},{12,8},{1,5},{5,1},{9,13},{13,9},{2,6},{6,2},{1... | collective-permute-start | bytes 786440 | tf_op jit(solution)/shard_map/ppermute | solution.py:10
  70.2 11.4 %collective-permute-start.2 = (f32[256,256]{1,0:T(8,128)S(1)}, f32[256,256]{1,0:T(8,128)S(1)}, u32[]{:S(2)}, u32[]{:S(2)}) collective-permute-start(f32[256,256]{1,0:T(8,128)S(1)} %add.117), channel_id=1, source_target_pairs={{0,8},{4,12},{8,0},{12,4},{1,9},{5,13},{9,1},{13,5},{2,10},{6,14},... | collective-permute-start | bytes 786440 | tf_op jit(solution)/shard_map/ppermute | solution.py:10
  82.0 6.4 %collective-permute-start.3 = (f32[256,256]{0,1:T(8,128)S(1)}, f32[256,256]{0,1:T(8,128)S(1)}, u32[]{:S(2)}, u32[]{:S(2)}) collective-permute-start(f32[256,256]{0,1:T(8,128)S(1)} %convolution_bitcast_fusion.1), channel_id=1, source_target_pairs={{0,4},{4,0},{8,12},{12,8},{1,5},{5,1},{9,13},{13,9},{2,6},{6,2},{1... | collective-permute-start | bytes 786440 | tf_op jit(solution)/shard_map/ppermute | solution.py:10
  88.5 12.7 %collective-permute-start.4 = (f32[256,256]{0,1:T(8,128)S(1)}, f32[256,256]{0,1:T(8,128)S(1)}, u32[]{:S(2)}, u32[]{:S(2)}) collective-permute-start(f32[256,256]{0,1:T(8,128)S(1)} %add.119), channel_id=1, source_target_pairs={{0,8},{4,12},{8,0},{12,4},{1,9},{5,13},{9,1},{13,5},{2,10},{6,14},... | collective-permute-start | bytes 786440 | tf_op jit(solution)/shard_map/ppermute | solution.py:10
  101.2 12.6 %copy-start.4 = (bf16[256,1024]{1,0:T(8,128)(2,1)S(1)}, bf16[256,1024]{1,0:T(8,128)(2,1)}, u32[]{:S(2)}) copy-start(bf16[256,1024]{1,0:T(8,128)(2,1)} %copy-done.3) | copy-start | bytes 1572868
  103.3 7.3 %collective-permute-start.5 = (f32[256,256]{0,1:T(8,128)S(1)}, f32[256,256]{0,1:T(8,128)S(1)}, u32[]{:S(2)}, u32[]{:S(2)}) collective-permute-start(f32[256,256]{0,1:T(8,128)S(1)} %convolution_bitcast_fusion), channel_id=1, source_target_pairs={{0,4},{4,0},{8,12},{12,8},{1,5},{5,1},{9,13},{13,9},{2,6},{6,2},{1... | collective-permute-start | bytes 786440 | tf_op jit(solution)/shard_map/ppermute | solution.py:10
  120.9 61.5 %copy-start.1 = (bf16[1024,256]{1,0:T(8,128)(2,1)}, bf16[1024,256]{1,0:T(8,128)(2,1)S(1)}, u32[]{:S(2)}) copy-start(bf16[1024,256]{1,0:T(8,128)(2,1)S(1)} %scatter_custom_fusion.3) | copy-start | bytes 1572868
Sparse Core Ops, SparseCore 0:
  18.1 34.6 all-reduce.1
  124.0 58.4 reduce-scatter.3
where the time goes:
time: 190 us; the launch traced here: 189 us
  waiting for transfers between devices  125 us (66%)
  local copies, waits for them, and re-layouts  19 us (10%)
  between operations  15.2 us (8%)
  starting transfers between devices  11.1 us (6%)
  matrix products  9.46 us (5%)
  blocking collectives  7.19 us (4%)
  other arithmetic  2.34 us (1%)
    unnamed x3, waiting for transfers between devices  58.6 us
    ppermute x6, waiting for transfers between devices, partner(): return lax.ppermute(value, axis, pairs)  39.9 us
    psum x1, waiting for transfers between devices, shards(): summed = lax.psum(spread, ('rhs', 'pan'))  26.5 us
    ppermute x6, starting transfers between devices, partner(): return lax.ppermute(value, axis, pairs)  11 us
    all_gather x1, blocking collectives, shards(): loads = lax.all_gather(upper_source, ('rhs', 'pan'), axis=1, tiled=True)  7.19 us
    scatter x1, local copies, waits for them, and re-layouts, shards(): adjoint = jnp.zeros_like(bottom_back).at[order_rows].set(bottom_back)  5.07 us
    gather x1, local copies, waits for them, and re-layouts, shards(): ordered = bottom_source[order_rows] * row_mask  4.57 us
  transfers between devices with their start and end apart: 8, of which 8 were waited for; matrix products, arithmetic and copies ran while one was open for 1% of the time, Pallas kernels for 0%

commit v1 on v0

v1 whole, which is shorter than its diff:
```python
import functools

import jax
import jax.numpy as jnp
from jax import lax
from jax.experimental import pallas as pl
from jax.experimental.pallas import tpu as pltpu
from jax.sharding import PartitionSpec as P

MESH = pl.DeviceIdType.MESH
F32 = jnp.float32
BF16 = jnp.bfloat16
LANES = 128
PLAIN = ((1,), (0,))
RIGHT_T = ((1,), (1,))
LEFT_T = ((0,), (0,))


def mul(a, b, dims=PLAIN):
    return lax.dot_general(a, b, (dims, ((), ())), preferred_element_type=F32)


def one_hot(rows, keys):
    shape = (rows, keys.shape[1])
    hit = lax.broadcasted_iota(jnp.int32, shape, 0) == keys
    return jnp.where(hit, 1.0, 0.0).astype(BF16)


def kernel(
    sizes,
    src_h, inv_h, upd_h, sen_h, ord_h, ext_h, tgt_h, us_h, ui_h, uc_h, ut_h,
    adj_h, grad_ref,
    src, inv, upd, sen, order, extent, target, us0, ui, uc, ut,
    local_sem,
    nhot, spread_upd, solved, ordered, adj,
    hi, us, iv, cp, ld, zed,
    sp, pr, lf, ba, back_own, gs, gr, gh, gz,
    hi_s, hi_r, rel_s, rel_r, us_s, us_r, pr_s, pr_r, lf_s, lf_r, ba_s, ba_r, gr_s, gr_r, gz_s, gz_r,
):
    leaves, rhs, pan, front, rows_each = sizes
    members = rhs * pan
    depth = leaves.bit_length() - 1
    rows = inv.shape[0]
    width = us.shape[2]
    f = lax.axis_index("leaf")
    x = lax.axis_index("rhs")
    c = lax.axis_index("pan")
    j = x * pan + c
    half = front // 2
    inv_rows = ui.shape[0] - front
    cut = uc.shape[0] // 2
    strips = (hi.shape[1] - inv_rows) // cut
    upper_cols = uc.shape[1] - front

    def member(k):
        return lax.rem(j + k, members)

    def leaf(k):
        return lax.rem(f + k, leaves)

    def at_member(k):
        place = member(k)
        return {"rhs": place // pan, "pan": lax.rem(place, pan)}

    def at_leaf(k):
        return {"leaf": leaf(k)}

    def copy(a, b, s, r, to):
        return pltpu.make_async_remote_copy(
            src_ref=a, dst_ref=b, send_sem=s, recv_sem=r, device_id=to, device_id_type=MESH
        )

    fetch = {}
    for place, (name, a, b) in enumerate((
        ("ui", ui_h, ui), ("uc", uc_h, uc), ("order", ord_h, order), ("extent", ext_h, extent),
        ("target", tgt_h, target), ("ut", ut_h, ut), ("upd", upd_h, upd), ("src", src_h, src),
        ("inv", inv_h, inv), ("us0", us_h, us0), ("sen", sen_h, sen),
    )):
        fetch[name] = pltpu.make_async_copy(a, b, local_sem.at[place])
        fetch[name].start()

    barrier = pltpu.get_barrier_semaphore()
    for k in range(1, members):
        pl.semaphore_signal(barrier, inc=1, device_id=at_member(k), device_id_type=MESH)
    for k in range(1, leaves):
        pl.semaphore_signal(barrier, inc=1, device_id=at_leaf(k), device_id_type=MESH)
    pl.semaphore_wait(barrier, members + leaves - 2)

    fetch["ui"].wait()
    fetch["uc"].wait()
    for side in range(2):
        slot = side * leaves + f
        hi[slot, 0:inv_rows, :] = ui[front:, side * half : (side + 1) * half]
        for strip in range(strips):
            start = inv_rows + strip * cut
            have = min(LANES, upper_cols - strip * LANES)
            piece = uc[side * cut : (side + 1) * cut, front + strip * LANES : front + strip * LANES + have]
            if have < LANES:
                piece = jnp.concatenate([piece, jnp.zeros((cut, LANES - have), BF16)], axis=1)
            hi[slot, start : start + cut, :] = piece
    mine = c * leaves + f
    sends = []
    for k in range(1, leaves):
        out = copy(hi.at[mine], hi.at[mine], hi_s.at[k], hi_r.at[f], at_leaf(k))
        out.start()
        sends.append(out)
    fetch["us0"].wait()
    us[f] = us0[front:, :]
    for k in range(1, leaves):
        out = copy(us.at[f], us.at[f], us_s.at[k], us_r.at[f], at_leaf(k))
        out.start()
        sends.append(out)

    for name in ("order", "extent", "target", "ut"):
        fetch[name].wait()
    used = lax.broadcasted_iota(jnp.int32, (1, rows), 1) < extent[0]
    keys = jnp.where(used, order[...], -1)
    for start in range(0, rows, 256):
        hit = lax.broadcasted_iota(jnp.int32, (256, rows), 0) + start == keys
        nhot[start : start + 256, :] = jnp.where(hit, 1.0, 0.0).astype(BF16)
    fetch["src"].wait()
    ordered[...] = mul(src[...], nhot[...], LEFT_T).astype(BF16)
    fetch["upd"].wait()
    spread_upd[...] = mul(one_hot(front, target[...]), upd[...]).astype(BF16)
    fetch["inv"].wait()
    for start in range(0, rows, 256):
        end = start + 256
        block = mul(ordered[:, :end], inv[start:end, :end], RIGHT_T)
        solved[:, start:end] = jnp.where(used[:, start:end], block, 0.0).astype(BF16)
    sp[...] = mul(solved[...], spread_upd[...], RIGHT_T).astype(BF16)
    for k in range(1, members):
        to = pl.multiple_of(member(k) * width, width)
        out = copy(sp.at[pl.ds(to, width)], pr.at[j], pr_s.at[k], pr_r.at[j], at_member(k))
        out.start()
        sends.append(out)
    pr[j] = sp[pl.ds(pl.multiple_of(j * width, width), width), :]

    eye = one_hot(front, lax.broadcasted_iota(jnp.int32, (1, front), 1))
    load_own = mul(us0[:front, :], eye, LEFT_T)
    map_own = one_hot(front, ut[pl.ds(f, 1), :])
    cp_own = mul(map_own, uc[:, :front]).astype(BF16)
    inv_own = ui[:front, :]

    for k in range(1, members):
        place = member(k)
        copy(pr.at[place], pr.at[place], pr_s.at[k], pr_r.at[place], at_member(k)).wait_recv()
    total = pr[0].astype(F32)
    for place in range(1, members):
        total = total + pr[place].astype(F32)
    front_in = (load_own - total).astype(BF16)
    zed_own = mul(front_in, inv_own, RIGHT_T).astype(BF16)
    lf[f] = mul(zed_own, cp_own, RIGHT_T).astype(BF16)
    for k in range(1, leaves):
        out = copy(lf.at[f], lf.at[f], lf_s.at[k], lf_r.at[f], at_leaf(k))
        out.start()
        sends.append(out)

    for k in range(1, leaves):
        slot = c * leaves + leaf(k)
        copy(hi.at[slot], hi.at[slot], hi_s.at[k], hi_r.at[leaf(k)], at_leaf(k)).wait_recv()
        out = copy(hi.at[slot], hi.at[slot], rel_s.at[k], rel_r.at[leaf(k)], {"pan": 1 - c})
        out.start()
        sends.append(out)
    for k in range(1, leaves):
        slot = leaf(k)
        copy(us.at[slot], us.at[slot], us_s.at[k], us_r.at[slot], at_leaf(k)).wait_recv()
    for k in range(1, leaves):
        slot = (1 - c) * leaves + leaf(k)
        copy(hi.at[slot], hi.at[slot], rel_s.at[k], rel_r.at[leaf(k)], {"pan": 1 - c}).wait_recv()

    first = {}
    count = 0
    for height in range(1, depth + 1):
        first[height] = count
        count += leaves >> height
    for height in range(1, depth + 1):
        n = front >> height
        o = front - (2 * front >> height)
        for p in range(leaves >> height):
            at = first[height] + p
            group = [p * (1 << height) + s for s in range(1 << height)]
            for s, g in enumerate(group):
                for side in range(2):
                    iv[at, s * n : (s + 1) * n, side * half : (side + 1) * half] = hi[
                        side * leaves + g, o : o + n, :
                    ]
            stacked = jnp.concatenate([us[g, o : o + n, :] for g in group], axis=0)
            ld[at] = mul(stacked, eye, LEFT_T)
            if height < depth:
                pieces = []
                for s, g in enumerate(group):
                    strip_list = [
                        jnp.concatenate(
                            [
                                hi[side * leaves + g, inv_rows + strip * cut : inv_rows + (strip + 1) * cut, :]
                                for side in range(2)
                            ],
                            axis=0,
                        )
                        for strip in range(strips)
                    ]
                    if n % LANES == 0 and o % LANES == 0:
                        pieces.extend(strip_list[o // LANES : (o + n) // LANES])
                    else:
                        whole = jnp.concatenate(strip_list, axis=1)
                        line = lax.broadcasted_iota(jnp.int32, (1, front), 1) - s * n
                        line = jnp.where((line >= 0) & (line < n), line + o, -1)
                        part = mul(whole, one_hot(whole.shape[1], line))
                        pieces = [part + pieces[0]] if pieces else [part]
                coup = jnp.concatenate(pieces, axis=1) if len(pieces) > 1 else pieces[0]
                map_row = 2 * leaves - (2 * leaves >> height) + p
                cp[at] = mul(one_hot(front, ut[map_row : map_row + 1, :]), coup.astype(BF16)).astype(BF16)

    for k in range(1, leaves):
        slot = leaf(k)
        copy(lf.at[slot], lf.at[slot], lf_s.at[k], lf_r.at[slot], at_leaf(k)).wait_recv()
    lifts = [lf[g].astype(F32) for g in range(leaves)]
    for height in range(1, depth + 1):
        above = []
        for p in range(leaves >> height):
            at = first[height] + p
            now = (ld[at] - (lifts[2 * p] + lifts[2 * p + 1])).astype(BF16)
            value = mul(now, iv[at], RIGHT_T).astype(BF16)
            zed[at] = value
            if height < depth:
                above.append(mul(value, cp[at], RIGHT_T))
        lifts = above
    back = mul(zed[first[depth]], iv[first[depth]]).astype(BF16)
    for height in range(depth - 1, 0, -1):
        at = first[height] + f // (1 << height)
        residue = (zed[at].astype(F32) - mul(back, cp[at])).astype(BF16)
        back = mul(residue, iv[at]).astype(BF16)
    residue = (zed_own.astype(F32) - mul(back, cp_own)).astype(BF16)
    back_own[...] = mul(residue, inv_own).astype(BF16)
    own_rows = pl.ds(pl.multiple_of(j * width, width), width)
    for k in range(1, members):
        out = copy(back_own, ba.at[own_rows], ba_s.at[k], ba_r.at[j], at_member(k))
        out.start()
        sends.append(out)
    ba[own_rows, :] = back_own[...]
    for k in range(1, members):
        place = member(k)
        here = ba.at[pl.ds(pl.multiple_of(place * width, width), width)]
        copy(here, here, ba_s.at[k], ba_r.at[place], at_member(k)).wait_recv()

    for start in range(0, rows, 256):
        end = start + 256
        value = solved[:, start:end].astype(F32) - mul(ba[...], spread_upd[:, start:end])
        ordered[:, start:end] = jnp.where(used[:, start:end], value, 0.0).astype(BF16)
    for start in range(0, rows, 256):
        end = start + 256
        block = mul(ordered[:, start:], inv[start:, start:end])
        solved[:, start:end] = jnp.where(used[:, start:end], block, 0.0).astype(BF16)
    adj[...] = mul(nhot[...], solved[...], RIGHT_T).astype(BF16)
    store = pltpu.make_async_copy(adj, adj_h, local_sem.at[11])
    store.start()
    fetch["sen"].wait()
    grad = -mul(sen[...], adj[...])
    tail = gs.shape[2] - rows_each
    for place in range(members):
        for g in range(leaves):
            start = (g * members + place) * rows_each
            piece = grad[start : start + rows_each]
            if tail:
                piece = jnp.concatenate([piece, jnp.zeros((tail, piece.shape[1]), F32)], axis=0)
            gs[place, g] = piece.astype(BF16)
    for k in range(1, members):
        out = copy(gs.at[member(k)], gr.at[j], gr_s.at[k], gr_r.at[j], at_member(k))
        out.start()
        sends.append(out)
    gr[j] = gs[j]
    for k in range(1, members):
        place = member(k)
        copy(gr.at[place], gr.at[place], gr_s.at[k], gr_r.at[place], at_member(k)).wait_recv()
    summed = gr[0].astype(F32)
    for place in range(1, members):
        summed = summed + gr[place].astype(F32)
    gh[...] = summed
    for k in range(1, leaves):
        out = copy(gh.at[leaf(k)], gz.at[f], gz_s.at[k], gz_r.at[f], at_leaf(k))
        out.start()
        sends.append(out)
    gz[f] = gh[f]
    for k in range(1, leaves):
        slot = leaf(k)
        copy(gz.at[slot], gz.at[slot], gz_s.at[k], gz_r.at[slot], at_leaf(k)).wait_recv()
    summed = gz[0]
    for g in range(1, leaves):
        summed = summed + gz[g]
    grad_ref[...] = summed[:rows_each]
    for out in sends:
        out.wait_send()
    store.wait()


def shards(*arrays):
    (src, inv, upd, sen, order, extent, target, us, ui, uc, ut) = arrays
    leaves, rhs, pan = (lax.axis_size(name) for name in ("leaf", "rhs", "pan"))
    members = rhs * pan
    front = ui.shape[1]
    rows, cols = src.shape
    width = cols // members
    rows_each = sen.shape[0] // (leaves * members)
    rows_kept = -(-rows_each // 16) * 16
    upper_rows = ui.shape[0] - front
    strips = -(-(uc.shape[1] - front) // LANES)
    hi_rows = upper_rows + strips * (uc.shape[0] // 2)
    above = leaves - 1

    def room(shape, kind=BF16):
        return pltpu.VMEM(shape, kind)

    scratch = [
        room(src.shape), room(inv.shape), room(upd.shape), room(sen.shape),
        room(order.shape, jnp.int32), pltpu.SMEM(extent.shape, jnp.int32), room(target.shape, jnp.int32),
        room(us.shape), room(ui.shape), room(uc.shape), room(ut.shape, jnp.int32),
        pltpu.SemaphoreType.DMA((12,)),
        room((rows, rows)), room((front, rows)), room((cols, rows)), room((cols, rows)), room((rows, cols)),
        room((2 * leaves, hi_rows, LANES)), room((leaves, upper_rows, width)),
        room((above, front, front)), room((above, front, front)),
        room((above, width, front), F32), room((above, width, front)),
        room((cols, front)), room((members, width, front)), room((leaves, width, front)),
        room((cols, front)), room((width, front)),
        room((members, leaves, rows_kept, cols)), room((members, leaves, rows_kept, cols)),
        room((leaves, rows_kept, cols), F32), room((leaves, rows_kept, cols), F32),
    ]
    for count in (leaves, leaves, leaves, members, leaves, members, members, leaves):
        scratch += [pltpu.SemaphoreType.DMA((count,))] * 2
    any_spec = pl.BlockSpec(memory_space=pl.ANY)
    flops = 2 * rows * rows * cols * 4
    return pl.pallas_call(
        functools.partial(kernel, (leaves, rhs, pan, front, rows_each)),
        out_shape=(
            jax.ShapeDtypeStruct(src.shape, BF16),
            jax.ShapeDtypeStruct((rows_each, cols), F32),
        ),
        in_specs=[any_spec] * 11,
        out_specs=(any_spec, pl.BlockSpec(memory_space=pltpu.VMEM)),
        scratch_shapes=scratch,
        compiler_params=pltpu.CompilerParams(
            collective_id=0, has_side_effects=True, vmem_limit_bytes=56 * 2**20
        ),
        cost_estimate=pl.CostEstimate(flops=flops, bytes_accessed=5 * 2**20, transcendentals=0),
    )(*arrays)


def solution(mesh):
    placed = (
        P(("rec", "leaf", "rhs", "pan"), None),
        P(("rec", "leaf", "rhs", "pan"), None),
        P(("rec", "leaf", "rhs", "pan"), None),
        P("rec", ("leaf", "rhs", "pan")),
        P(("leaf", "rhs", "pan"), None),
        P(("leaf", "rhs", "pan")),
        P(("leaf", "rhs", "pan"), None),
        P(("rec", "leaf"), ("rhs", "pan")),
        P(("rec", "leaf"), None),
        P("rec", "leaf"),
        P(),
    )
    return jax.shard_map(
        shards,
        mesh=mesh,
        in_specs=placed,
        out_specs=(P(("rec", "leaf", "rhs", "pan"), None), P(("rec", "leaf", "rhs", "pan"), None)),
        check_vma=False,
    )
```

time: 190 us -> 41.3 us (0.22)
  waiting for transfers between devices: 125 us -> 0 us
  Pallas kernels: 0 us -> 34.9 us
  local copies, waits for them, and re-layouts: 19 us -> 4.85 us
  between operations: 15.2 us -> 1.29 us
  starting transfers between devices: 11.1 us -> 0 us
  matrix products: 9.46 us -> 0 us
  blocking collectives: 7.19 us -> 0 us
  other arithmetic: 2.34 us -> 0 us
    unnamed x3 -> x0, waiting for transfers between devices: 58.6 us -> none
    ppermute x6 -> x0, waiting for transfers between devices: 39.9 us -> none  [partner(): return lax.ppermute(value, axis, pairs)]
    pallas_call x0 -> x1, Pallas kernels: none -> 34.9 us  [shards(): pl.pallas_call(functools.partial(kernel, (leaves, rhs, pan, front, rows_e...]
    psum x1 -> x0, waiting for transfers between devices: 26.5 us -> none  [shards(): summed = lax.psum(spread, ('rhs', 'pan'))]
    ppermute x6 -> x0, starting transfers between devices: 11 us -> none  [partner(): return lax.ppermute(value, axis, pairs)]
    dot_general x11 -> x0, matrix products: 9.46 us -> none  [the longest x3 2.68 us: shards(): jnp.einsum('ij,ic->jc', inverse_now, residue, preferred_element_type=jnp....]
    scatter x4 -> x0, local copies, waits for them, and re-layouts: 8.91 us -> none  [the longest x1 5.07 us: shards(): adjoint = jnp.zeros_like(bottom_back).at[order_rows].set(bottom_back)]
    all_gather x1 -> x0, blocking collectives: 7.19 us -> none  [shards(): loads = lax.all_gather(upper_source, ('rhs', 'pan'), axis=1, tiled=True)]
  transfers between devices with their start and end apart: 8 -> 0, of which waited for: 8 -> 0; matrix products, arithmetic and copies ran while one was open for 1% -> 0% of each run, Pallas kernels for 0% -> 0%
where the time goes in v1:
time: 41.3 us; the launch traced here: 41 us
  Pallas kernels  34.9 us (85%)
  local copies, waits for them, and re-layouts  4.85 us (12%)
  between operations  1.29 us (3%)
    pallas_call x1, Pallas kernels, shards(): pl.pallas_call(functools.partial(kernel, (leaves, rhs, pan, front, rows_e...  34.9 us
    unnamed x3, local copies, waits for them, and re-layouts  4.85 us

profile of v1, /device:TPU:0, one launch (start us, length us, event | category | flops | bytes accessed | tf_op | source)
XLA Modules:
  0.0 41.0 jit_solution(16516672646335338381)
XLA Ops:
  1.3 1.6 %copy.13.us_h = bf16[448,64]{1,0:T(8,128)(2,1)} copy(bf16[448,64]{0,1:T(8,128)(2,1)} %param.18) | data formatting | bytes 114688 | tf_op args[7]
  2.9 34.9 %shard_map.122 = (bf16[1024,256]{1,0:T(8,128)(2,1)}, f32[32,256]{1,0:T(8,128)}) custom-call(bf16[1024,256]{1,0:T(8,128)(2,1)} %src_h.1, bf16[1024,1024]{1,0:T(8,128)(2,1)} %inv_h.1, bf16[128,1024]{1,0:T(8,128)(2,1)} %upd_h.1, bf16[512,1024]{1,0:T(8,128)(2,1)} %sen_h.1, s32[1,1024]{1,0:T(1,128)} %ord_h.1, s32[1]{0:T(128)S(6)} %copy.16.ext_h, s32[1,128]{1,0:T(1,128)} %tgt_h.1, ...), custom_call_target="tpu_custom_call" | custom-call | flops 2147483648 | bytes 5242880 | tf_op jit(solution)/shard_map/pallas_call | solution.py:331
  37.8 1.9 %copy.17 = bf16[1024,256]{1,0:T(8,128)(2,1)} copy(bf16[1024,256]{1,0:T(8,128)(2,1)} %get-tuple-element.4) | data formatting | bytes 1048576
  39.6 1.4 %copy.18 = f32[32,256]{1,0:T(8,128)} copy(f32[32,256]{1,0:T(8,128)} %get-tuple-element.5) | data formatting | bytes 65536

commit v2 on v1

--- a/solution.py
+++ b/solution.py
@@ -35,13 +35,13 @@
     nhot, spread_upd, solved, ordered, adj,
     hi, us, iv, cp, ld, zed,
     sp, pr, lf, ba, back_own, gs, gr, gh, gz,
-    hi_s, hi_r, rel_s, rel_r, us_s, us_r, pr_s, pr_r, lf_s, lf_r, ba_s, ba_r, gr_s, gr_r, gz_s, gz_r,
+    hi_s, hi_r, row_s, row_r, rel_s, rel_r, us_s, us_r, pr_s, pr_r, lf_s, lf_r, ba_s, ba_r, gr_s, gr_r, gz_s, gz_r,
 ):
     leaves, rhs, pan, front, rows_each = sizes
     members = rhs * pan
     depth = leaves.bit_length() - 1
     rows = inv.shape[0]
-    width = us.shape[2]
+    width = us.shape[1]
     f = lax.axis_index("leaf")
     x = lax.axis_index("rhs")
     c = lax.axis_index("pan")
@@ -49,8 +49,9 @@
     half = front // 2
     inv_rows = ui.shape[0] - front
     cut = uc.shape[0] // 2
-    strips = (hi.shape[1] - inv_rows) // cut
     upper_cols = uc.shape[1] - front
+    strips = -(-upper_cols // LANES)
+    part = hi.shape[1] // rhs
 
     def member(k):
         return lax.rem(j + k, members)
@@ -98,14 +99,20 @@
             if have < LANES:
                 piece = jnp.concatenate([piece, jnp.zeros((cut, LANES - have), BF16)], axis=1)
             hi[slot, start : start + cut, :] = piece
-    mine = c * leaves + f
+        start = inv_rows + strips * cut
+        if start < hi.shape[1]:
+            hi[slot, start:, :] = jnp.zeros((hi.shape[1] - start, LANES), BF16)
     sends = []
-    for k in range(1, leaves):
-        out = copy(hi.at[mine], hi.at[mine], hi_s.at[k], hi_r.at[f], at_leaf(k))
+
+    def share(place):
+        return hi.at[c * leaves + place, pl.ds(pl.multiple_of(x * part, part), part)]
+
+    for k in range(1, leaves):
+        out = copy(share(f), share(f), hi_s.at[k], hi_r.at[f], at_leaf(k))
         out.start()
         sends.append(out)
     fetch["us0"].wait()
-    us[f] = us0[front:, :]
+    us[f] = us0[:, front:]
     for k in range(1, leaves):
         out = copy(us.at[f], us.at[f], us_s.at[k], us_r.at[f], at_leaf(k))
         out.start()
@@ -135,11 +142,18 @@
         sends.append(out)
     pr[j] = sp[pl.ds(pl.multiple_of(j * width, width), width), :]
 
-    eye = one_hot(front, lax.broadcasted_iota(jnp.int32, (1, front), 1))
-    load_own = mul(us0[:front, :], eye, LEFT_T)
+    load_own = us0[:, :front].astype(F32)
     map_own = one_hot(front, ut[pl.ds(f, 1), :])
     cp_own = mul(map_own, uc[:, :front]).astype(BF16)
     inv_own = ui[:front, :]
+
+    for k in range(1, leaves):
+        g = leaf(k)
+        copy(share(g), share(g), hi_s.at[k], hi_r.at[g], at_leaf(k)).wait_recv()
+        for t in range(1, rhs):
+            out = copy(share(g), share(g), row_s.at[t, k], row_r.at[x, g], {"rhs": lax.rem(x + t, rhs)})
+            out.start()
+            sends.append(out)
 
     for k in range(1, members):
         place = member(k)
@@ -157,7 +171,10 @@
 
     for k in range(1, leaves):
         slot = c * leaves + leaf(k)
-        copy(hi.at[slot], hi.at[slot], hi_s.at[k], hi_r.at[leaf(k)], at_leaf(k)).wait_recv()
+        for t in range(1, rhs):
+            other = lax.rem(x + t, rhs)
+            here = hi.at[slot, pl.ds(pl.multiple_of(other * part, part), part)]
+            copy(here, here, row_s.at[t, k], row_r.at[other, leaf(k)], {"rhs": other}).wait_recv()
         out = copy(hi.at[slot], hi.at[slot], rel_s.at[k], rel_r.at[leaf(k)], {"pan": 1 - c})
         out.start()
         sends.append(out)
@@ -184,8 +201,15 @@
                     iv[at, s * n : (s + 1) * n, side * half : (side + 1) * half] = hi[
                         side * leaves + g, o : o + n, :
                     ]
-            stacked = jnp.concatenate([us[g, o : o + n, :] for g in group], axis=0)
-            ld[at] = mul(stacked, eye, LEFT_T)
+            if n % LANES == 0 and o % LANES == 0:
+                ld[at] = jnp.concatenate([us[g, :, o : o + n] for g in group], axis=1).astype(F32)
+            else:
+                load = jnp.zeros(ld.shape[1:], F32)
+                for s, g in enumerate(group):
+                    line = lax.broadcasted_iota(jnp.int32, (1, front), 1) - s * n
+                    line = jnp.where((line >= 0) & (line < n), line + o, -1)
+                    load = load + mul(us[g], one_hot(us.shape[2], line))
+                ld[at] = load
             if height < depth:
                 pieces = []
                 for s, g in enumerate(group):
@@ -205,8 +229,8 @@
                         whole = jnp.concatenate(strip_list, axis=1)
                         line = lax.broadcasted_iota(jnp.int32, (1, front), 1) - s * n
                         line = jnp.where((line >= 0) & (line < n), line + o, -1)
-                        part = mul(whole, one_hot(whole.shape[1], line))
-                        pieces = [part + pieces[0]] if pieces else [part]
+                        gain = mul(whole, one_hot(whole.shape[1], line))
+                        pieces = [gain + pieces[0]] if pieces else [gain]
                 coup = jnp.concatenate(pieces, axis=1) if len(pieces) > 1 else pieces[0]
                 map_row = 2 * leaves - (2 * leaves >> height) + p
                 cp[at] = mul(one_hot(front, ut[map_row : map_row + 1, :]), coup.astype(BF16)).astype(BF16)
@@ -275,7 +299,7 @@
     summed = gr[0].astype(F32)
     for place in range(1, members):
         summed = summed + gr[place].astype(F32)
-    gh[...] = summed
+    gh[...] = summed.astype(BF16)
     for k in range(1, leaves):
         out = copy(gh.at[leaf(k)], gz.at[f], gz_s.at[k], gz_r.at[f], at_leaf(k))
         out.start()
@@ -284,17 +308,36 @@
     for k in range(1, leaves):
         slot = leaf(k)
         copy(gz.at[slot], gz.at[slot], gz_s.at[k], gz_r.at[slot], at_leaf(k)).wait_recv()
-    summed = gz[0]
+    summed = gz[0].astype(F32)
     for g in range(1, leaves):
-        summed = summed + gz[g]
+        summed = summed + gz[g].astype(F32)
     grad_ref[...] = summed[:rows_each]
     for out in sends:
         out.wait_send()
     store.wait()
 
 
+def hand_on(adj, grad, adj_out, grad_out, adj_held, grad_held, sem):
+    step = adj.shape[0] // 4
+    parts = [(grad, grad_held, grad_out)]
+    for start in range(0, adj.shape[0], step):
+        rows = pl.ds(start, step)
+        parts.append((adj.at[rows], adj_held.at[rows], adj_out.at[rows]))
+    moves = []
+    for place, (a, b, to) in enumerate(parts):
+        come = pltpu.make_async_copy(a, b, sem.at[0, place])
+        come.start()
+        moves.append((come, pltpu.make_async_copy(b, to, sem.at[1, place])))
+    for come, go in moves:
+        come.wait()
+        go.start()
+    for come, go in moves:
+        go.wait()
+
+
 def shards(*arrays):
     (src, inv, upd, sen, order, extent, target, us, ui, uc, ut) = arrays
+    us = us.T
     leaves, rhs, pan = (lax.axis_size(name) for name in ("leaf", "rhs", "pan"))
     members = rhs * pan
     front = ui.shape[1]
@@ -304,7 +347,7 @@
     rows_kept = -(-rows_each // 16) * 16
     upper_rows = ui.shape[0] - front
     strips = -(-(uc.shape[1] - front) // LANES)
-    hi_rows = upper_rows + strips * (uc.shape[0] // 2)
+    hi_rows = -(-(upper_rows + strips * (uc.shape[0] // 2)) // (16 * rhs)) * 16 * rhs
     above = leaves - 1
 
     def room(shape, kind=BF16):
@@ -316,19 +359,20 @@
         room(us.shape), room(ui.shape), room(uc.shape), room(ut.shape, jnp.int32),
         pltpu.SemaphoreType.DMA((12,)),
         room((rows, rows)), room((front, rows)), room((cols, rows)), room((cols, rows)), room((rows, cols)),
-        room((2 * leaves, hi_rows, LANES)), room((leaves, upper_rows, width)),
+        room((2 * leaves, hi_rows, LANES)), room((leaves, width, upper_rows)),
         room((above, front, front)), room((above, front, front)),
         room((above, width, front), F32), room((above, width, front)),
         room((cols, front)), room((members, width, front)), room((leaves, width, front)),
         room((cols, front)), room((width, front)),
         room((members, leaves, rows_kept, cols)), room((members, leaves, rows_kept, cols)),
-        room((leaves, rows_kept, cols), F32), room((leaves, rows_kept, cols), F32),
+        room((leaves, rows_kept, cols)), room((leaves, rows_kept, cols)),
     ]
-    for count in (leaves, leaves, leaves, members, leaves, members, members, leaves):
-        scratch += [pltpu.SemaphoreType.DMA((count,))] * 2
+    for count in (leaves, (rhs, leaves), leaves, leaves, members, leaves, members, members, leaves):
+        count = count if isinstance(count, tuple) else (count,)
+        scratch += [pltpu.SemaphoreType.DMA(count)] * 2
     any_spec = pl.BlockSpec(memory_space=pl.ANY)
     flops = 2 * rows * rows * cols * 4
-    return pl.pallas_call(
+    held = pl.pallas_call(
         functools.partial(kernel, (leaves, rhs, pan, front, rows_each)),
         out_shape=(
             jax.ShapeDtypeStruct(src.shape, BF16),
@@ -341,7 +385,15 @@
             collective_id=0, has_side_effects=True, vmem_limit_bytes=56 * 2**20
         ),
         cost_estimate=pl.CostEstimate(flops=flops, bytes_accessed=5 * 2**20, transcendentals=0),
-    )(*arrays)
+    )(src, inv, upd, sen, order, extent, target, us, ui, uc, ut)
+    hbm = pl.BlockSpec(memory_space=pltpu.HBM)
+    return pl.pallas_call(
+        hand_on,
+        out_shape=tuple(jax.ShapeDtypeStruct(part.shape, part.dtype) for part in held),
+        in_specs=[hbm] * 2,
+        out_specs=(hbm, hbm),
+        scratch_shapes=[room(part.shape, part.dtype) for part in held] + [pltpu.SemaphoreType.DMA((2, 5))],
+    )(*held)
 
 
 def solution(mesh):

time: 41.3 us -> 35.6 us (0.86)
  local copies, waits for them, and re-layouts: 4.85 us -> 0 us
  Pallas kernels: 34.9 us -> 34.1 us
    unnamed x3 -> x0, local copies, waits for them, and re-layouts: 4.85 us -> none
    pallas_call x1, Pallas kernels: 34.9 us -> 32.3 us  [shards(): pl.pallas_call(functools.partial(kernel, (leaves, rhs, pan, front, rows_e...]
    pallas_call x0 -> x1, Pallas kernels: none -> 1.86 us  [shards(): pl.pallas_call(hand_on, out_shape=tuple((jax.ShapeDtypeStruct(part.shape,...]
where the time goes in v2:
time: 35.6 us; the launch traced here: 35.4 us
  Pallas kernels  34.1 us (96%)
  between operations  1.29 us (4%)
    pallas_call x1, Pallas kernels, shards(): pl.pallas_call(functools.partial(kernel, (leaves, rhs, pan, front, rows_e...  32.3 us
    pallas_call x1, Pallas kernels, shards(): pl.pallas_call(hand_on, out_shape=tuple((jax.ShapeDtypeStruct(part.shape,...  1.86 us

profile of v2, /device:TPU:0, one launch (start us, length us, event | category | flops | bytes accessed | tf_op | source)
XLA Modules:
  0.0 35.4 jit_solution(10201444153971374606)
XLA Ops:
  1.3 32.3 %shard_map.122 = (bf16[1024,256]{1,0:T(8,128)(2,1)}, f32[32,256]{1,0:T(8,128)}) custom-call(bf16[1024,256]{1,0:T(8,128)(2,1)} %src_h.1, bf16[1024,1024]{1,0:T(8,128)(2,1)} %inv_h.1, bf16[128,1024]{1,0:T(8,128)(2,1)} %upd_h.1, bf16[512,1024]{1,0:T(8,128)(2,1)} %sen_h.1, s32[1,1024]{1,0:T(1,128)} %ord_h.1, s32[1]{0:T(128)S(6)} %copy.13.ext_h, s32[1,128]{1,0:T(1,128)} %tgt_h.1, ...), custom_call_target="tpu_custom_call" | custom-call | flops 2147483648 | bytes 5242880 | tf_op jit(solution)/shard_map/pallas_call | solution.py:375
  33.6 1.9 %shard_map.123 = (bf16[1024,256]{1,0:T(8,128)(2,1)}, f32[32,256]{1,0:T(8,128)}) custom-call(bf16[1024,256]{1,0:T(8,128)(2,1)} %get-tuple-element.4.adj, f32[32,256]{1,0:T(8,128)} %get-tuple-element.5.grad), custom_call_target="tpu_custom_call" | custom-call | tf_op jit(solution)/shard_map/pallas_call | solution.py:390

commit v3 on v2

--- a/solution.py
+++ b/solution.py
@@ -34,7 +34,7 @@
     local_sem,
     nhot, spread_upd, solved, ordered, adj,
     hi, us, iv, cp, ld, zed,
-    sp, pr, lf, ba, back_own, gs, gr, gh, gz,
+    sp, pr, lf, ba, back_own, gk, gs, gr, gh, gz,
     hi_s, hi_r, row_s, row_r, rel_s, rel_r, us_s, us_r, pr_s, pr_r, lf_s, lf_r, ba_s, ba_r, gr_s, gr_r, gz_s, gz_r,
 ):
     leaves, rhs, pan, front, rows_each = sizes
@@ -78,14 +78,16 @@
         ("inv", inv_h, inv), ("us0", us_h, us0), ("sen", sen_h, sen),
     )):
         fetch[name] = pltpu.make_async_copy(a, b, local_sem.at[place])
-        fetch[name].start()
+        if name in ("ui", "uc", "us0"):
+            fetch[name].start()
 
     barrier = pltpu.get_barrier_semaphore()
     for k in range(1, members):
         pl.semaphore_signal(barrier, inc=1, device_id=at_member(k), device_id_type=MESH)
-    for k in range(1, leaves):
-        pl.semaphore_signal(barrier, inc=1, device_id=at_leaf(k), device_id_type=MESH)
-    pl.semaphore_wait(barrier, members + leaves - 2)
+    for k in range(rhs, leaves * rhs):
+        to = {"leaf": lax.rem(f + k // rhs, leaves), "rhs": lax.rem(x + k % rhs, rhs)}
+        pl.semaphore_signal(barrier, inc=1, device_id=to, device_id_type=MESH)
+    pl.semaphore_wait(barrier, members - 1 + (leaves - 1) * rhs)
 
     fetch["ui"].wait()
     fetch["uc"].wait()
@@ -117,6 +119,9 @@
         out = copy(us.at[f], us.at[f], us_s.at[k], us_r.at[f], at_leaf(k))
         out.start()
         sends.append(out)
+
+    for name in ("order", "extent", "target", "ut", "src", "upd", "inv", "sen"):
+        fetch[name].start()
 
     for name in ("order", "extent", "target", "ut"):
         fetch[name].wait()
@@ -280,37 +285,40 @@
     store.start()
     fetch["sen"].wait()
     grad = -mul(sen[...], adj[...])
-    tail = gs.shape[2] - rows_each
-    for place in range(members):
-        for g in range(leaves):
-            start = (g * members + place) * rows_each
-            piece = grad[start : start + rows_each]
-            if tail:
-                piece = jnp.concatenate([piece, jnp.zeros((tail, piece.shape[1]), F32)], axis=0)
-            gs[place, g] = piece.astype(BF16)
-    for k in range(1, members):
-        out = copy(gs.at[member(k)], gr.at[j], gr_s.at[k], gr_r.at[j], at_member(k))
-        out.start()
-        sends.append(out)
-    gr[j] = gs[j]
-    for k in range(1, members):
-        place = member(k)
-        copy(gr.at[place], gr.at[place], gr_s.at[k], gr_r.at[place], at_member(k)).wait_recv()
-    summed = gr[0].astype(F32)
-    for place in range(1, members):
-        summed = summed + gr[place].astype(F32)
-    gh[...] = summed.astype(BF16)
-    for k in range(1, leaves):
-        out = copy(gh.at[leaf(k)], gz.at[f], gz_s.at[k], gz_r.at[f], at_leaf(k))
-        out.start()
-        sends.append(out)
-    gz[f] = gh[f]
-    for k in range(1, leaves):
-        slot = leaf(k)
-        copy(gz.at[slot], gz.at[slot], gz_s.at[k], gz_r.at[slot], at_leaf(k)).wait_recv()
+    tail = gs.shape[1] - rows_each
+
+    def piece(g, place):
+        start = (g * members + place) * rows_each
+        value = grad[start : start + rows_each]
+        if tail:
+            value = jnp.concatenate([value, jnp.zeros((tail, value.shape[1]), F32)], axis=0)
+        return value
+
+    low = c == 0
+    for g in range(leaves):
+        for t in range(rhs):
+            one, two = piece(g, t * pan), piece(g, t * pan + 1)
+            gk[g * rhs + t] = jnp.where(low, one, two)
+            gs[g * rhs + t] = jnp.where(low, two, one).astype(BF16)
+    pair = copy(gs, gr, gr_s.at[0], gr_r.at[0], {"pan": 1 - c})
+    pair.start()
+    sends.append(pair)
+    pair.wait_recv()
+    gh[...] = (gk[...] + gr[...].astype(F32)).astype(BF16)
+    here = f * rhs + x
+    for k in range(1, leaves * rhs):
+        g, t = lax.rem(f + k // rhs, leaves), lax.rem(x + k % rhs, rhs)
+        out = copy(gh.at[g * rhs + t], gz.at[here], gz_s.at[k], gz_r.at[here], {"leaf": g, "rhs": t})
+        out.start()
+        sends.append(out)
+    gz[here] = gh[here]
+    for k in range(1, leaves * rhs):
+        g, t = lax.rem(f + k // rhs, leaves), lax.rem(x + k % rhs, rhs)
+        slot = g * rhs + t
+        copy(gz.at[slot], gz.at[slot], gz_s.at[k], gz_r.at[slot], {"leaf": g, "rhs": t}).wait_recv()
     summed = gz[0].astype(F32)
-    for g in range(1, leaves):
-        summed = summed + gz[g].astype(F32)
+    for slot in range(1, leaves * rhs):
+        summed = summed + gz[slot].astype(F32)
     grad_ref[...] = summed[:rows_each]
     for out in sends:
         out.wait_send()
@@ -364,13 +372,15 @@
         room((above, width, front), F32), room((above, width, front)),
         room((cols, front)), room((members, width, front)), room((leaves, width, front)),
         room((cols, front)), room((width, front)),
-        room((members, leaves, rows_kept, cols)), room((members, leaves, rows_kept, cols)),
-        room((leaves, rows_kept, cols)), room((leaves, rows_kept, cols)),
+        room((leaves * rhs, rows_kept, cols), F32), room((leaves * rhs, rows_kept, cols)),
+        room((leaves * rhs, rows_kept, cols)), room((leaves * rhs, rows_kept, cols)),
+        room((leaves * rhs, rows_kept, cols)),
     ]
-    for count in (leaves, (rhs, leaves), leaves, leaves, members, leaves, members, members, leaves):
+    for count in (leaves, (rhs, leaves), leaves, leaves, members, leaves, members, 1, leaves * rhs):
         count = count if isinstance(count, tuple) else (count,)
         scratch += [pltpu.SemaphoreType.DMA(count)] * 2
     any_spec = pl.BlockSpec(memory_space=pl.ANY)
+    hbm = pl.BlockSpec(memory_space=pltpu.HBM)
     flops = 2 * rows * rows * cols * 4
     held = pl.pallas_call(
         functools.partial(kernel, (leaves, rhs, pan, front, rows_each)),
@@ -386,7 +396,6 @@
         ),
         cost_estimate=pl.CostEstimate(flops=flops, bytes_accessed=5 * 2**20, transcendentals=0),
     )(src, inv, upd, sen, order, extent, target, us, ui, uc, ut)
-    hbm = pl.BlockSpec(memory_space=pltpu.HBM)
     return pl.pallas_call(
         hand_on,
         out_shape=tuple(jax.ShapeDtypeStruct(part.shape, part.dtype) for part in held),

time: 35.6 us -> 34.5 us (0.969)
  Pallas kernels: 34.1 us -> 33 us
    pallas_call x1, Pallas kernels: 32.3 us -> 31.1 us  [shards(): pl.pallas_call(functools.partial(kernel, (leaves, rhs, pan, front, rows_e...]
where the time goes in v3:
time: 34.5 us; the launch traced here: 34.3 us
  Pallas kernels  33 us (96%)
  between operations  1.29 us (4%)
    pallas_call x1, Pallas kernels, shards(): pl.pallas_call(functools.partial(kernel, (leaves, rhs, pan, front, rows_e...  31.1 us
    pallas_call x1, Pallas kernels, shards(): pl.pallas_call(hand_on, out_shape=tuple((jax.ShapeDtypeStruct(part.shape,...  1.86 us

profile of v3, /device:TPU:0, one launch (start us, length us, event | category | flops | bytes accessed | tf_op | source)
XLA Modules:
  0.0 34.3 jit_solution(15885993845004140318)
XLA Ops:
  1.3 31.1 %shard_map.122 = (bf16[1024,256]{1,0:T(8,128)(2,1)}, f32[32,256]{1,0:T(8,128)}) custom-call(bf16[1024,256]{1,0:T(8,128)(2,1)} %src_h.1, bf16[1024,1024]{1,0:T(8,128)(2,1)} %inv_h.1, bf16[128,1024]{1,0:T(8,128)(2,1)} %upd_h.1, bf16[512,1024]{1,0:T(8,128)(2,1)} %sen_h.1, s32[1,1024]{1,0:T(1,128)} %ord_h.1, s32[1]{0:T(128)S(6)} %copy.13.ext_h, s32[1,128]{1,0:T(1,128)} %tgt_h.1, ...), custom_call_target="tpu_custom_call" | custom-call | flops 2147483648 | bytes 5242880 | tf_op jit(solution)/shard_map/pallas_call | solution.py:385
  32.4 1.9 %shard_map.123 = (bf16[1024,256]{1,0:T(8,128)(2,1)}, f32[32,256]{1,0:T(8,128)}) custom-call(bf16[1024,256]{1,0:T(8,128)(2,1)} %get-tuple-element.4.adj, f32[32,256]{1,0:T(8,128)} %get-tuple-element.5.grad), custom_call_target="tpu_custom_call" | custom-call | tf_op jit(solution)/shard_map/pallas_call | solution.py:399

commit v4 on v3

--- a/solution.py
+++ b/solution.py
@@ -152,14 +152,6 @@
     cp_own = mul(map_own, uc[:, :front]).astype(BF16)
     inv_own = ui[:front, :]
 
-    for k in range(1, leaves):
-        g = leaf(k)
-        copy(share(g), share(g), hi_s.at[k], hi_r.at[g], at_leaf(k)).wait_recv()
-        for t in range(1, rhs):
-            out = copy(share(g), share(g), row_s.at[t, k], row_r.at[x, g], {"rhs": lax.rem(x + t, rhs)})
-            out.start()
-            sends.append(out)
-
     for k in range(1, members):
         place = member(k)
         copy(pr.at[place], pr.at[place], pr_s.at[k], pr_r.at[place], at_member(k)).wait_recv()
@@ -173,6 +165,14 @@
         out = copy(lf.at[f], lf.at[f], lf_s.at[k], lf_r.at[f], at_leaf(k))
         out.start()
         sends.append(out)
+
+    for k in range(1, leaves):
+        g = leaf(k)
+        copy(share(g), share(g), hi_s.at[k], hi_r.at[g], at_leaf(k)).wait_recv()
+        for t in range(1, rhs):
+            out = copy(share(g), share(g), row_s.at[t, k], row_r.at[x, g], {"rhs": lax.rem(x + t, rhs)})
+            out.start()
+            sends.append(out)
 
     for k in range(1, leaves):
         slot = c * leaves + leaf(k)

time: 34.5 us -> 34.9 us (1.012)
  Pallas kernels: 33 us -> 33.4 us
    pallas_call x1, Pallas kernels: 31.1 us -> 31.6 us  [shards(): pl.pallas_call(functools.partial(kernel, (leaves, rhs, pan, front, rows_e...]
where the time goes in v4:
time: 34.9 us; the launch traced here: 34.7 us
  Pallas kernels  33.4 us (96%)
  between operations  1.29 us (4%)
    pallas_call x1, Pallas kernels, shards(): pl.pallas_call(functools.partial(kernel, (leaves, rhs, pan, front, rows_e...  31.6 us
    pallas_call x1, Pallas kernels, shards(): pl.pallas_call(hand_on, out_shape=tuple((jax.ShapeDtypeStruct(part.shape,...  1.86 us

profile of v4, /device:TPU:0, one launch (start us, length us, event | category | flops | bytes accessed | tf_op | source)
XLA Modules:
  0.0 34.7 jit_solution(148081656772332360)
XLA Ops:
  1.3 31.6 %shard_map.122 = (bf16[1024,256]{1,0:T(8,128)(2,1)}, f32[32,256]{1,0:T(8,128)}) custom-call(bf16[1024,256]{1,0:T(8,128)(2,1)} %src_h.1, bf16[1024,1024]{1,0:T(8,128)(2,1)} %inv_h.1, bf16[128,1024]{1,0:T(8,128)(2,1)} %upd_h.1, bf16[512,1024]{1,0:T(8,128)(2,1)} %sen_h.1, s32[1,1024]{1,0:T(1,128)} %ord_h.1, s32[1]{0:T(128)S(6)} %copy.13.ext_h, s32[1,128]{1,0:T(1,128)} %tgt_h.1, ...), custom_call_target="tpu_custom_call" | custom-call | flops 2147483648 | bytes 5242880 | tf_op jit(solution)/shard_map/pallas_call | solution.py:385
  32.9 1.9 %shard_map.123 = (bf16[1024,256]{1,0:T(8,128)(2,1)}, f32[32,256]{1,0:T(8,128)}) custom-call(bf16[1024,256]{1,0:T(8,128)(2,1)} %get-tuple-element.4.adj, f32[32,256]{1,0:T(8,128)} %get-tuple-element.5.grad), custom_call_target="tpu_custom_call" | custom-call | tf_op jit(solution)/shard_map/pallas_call | solution.py:399
